TPU v7x, 32 devices: a whole 2x2x4 slice. The times are simulated.
32 devices in a mesh: groups: 2 (over x), gx: 8 (over z, y), gy: 2 (over core).
Axes of the slice: x: 2, y: 2, z: 4, core: 2. Of those that a mesh axis runs over, the one named last changes fastest.
Arguments:
- states: bfloat16 [384, 8192], P('groups', 'gx'), parts along dimension 0, may hold values from -6 to 6
- w_query: bfloat16 [8192, 8192], P('gx', 'gy'), may hold values from -0.0625 to 0.0625
- w_key_value: bfloat16 [8192, 2, 1024], P('gx', None, 'gy'), may hold values from -0.0625 to 0.0625
- w_out: bfloat16 [8192, 8192], P('gy', 'gx'), may hold values from -0.25 to 0.25
- cache_kv: bfloat16 [384, 2, 128, 1024], P(('groups', 'gx'), None, None, 'gy'), parts along dimension 0, may hold values from -140 to 140
- lengths: int32 [384], P(('groups', 'gx')), parts along dimension 0, may hold values from 1 to 128
- adapter_ids: int32 [384], P('groups'), parts along dimension 0, may hold values from 0 to 31, as said below
- placement: int32 [32], replicated, may hold values from 0 to 31, each once
- adapter_down: bfloat16 [32, 64, 8192], P('gx', None, 'gy'), may hold values from -0.25 to 0.25
- up_weight_slots: bfloat16 [32, 64, 8192], P(None, None, 'gx'), may hold values from -0.75 to 0.75
Outputs:
- output: bfloat16 [384, 8192], P(('groups', 'gy'), 'gx'), parts along dimension 0
There are 2 independent parts, one for each index of `groups`. A program takes and returns all parts, laid end to end along the dimension named above; an argument that names none is the same for every part. Nothing has to cross between parts.
Inputs may be any that keep to these rules, and one draw needn't show every extreme that they name: `adapter_ids`: in every aligned block of 24 rows, one adapter, the same in all blocks of a part, is named by exactly 2 rows; every other adapter is named by at most one row of a block, and some other adapter by one row of every block. `placement`: each slot holds one adapter; slot s lies with index s // (32 / 8) of gx.
All inputs are finite; a program needn't handle non-finite values.
Results may differ from a plain program's by a relative error of at most 0.012.
The roundings to bfloat16 on the way count: a program that leaves them out, or rounds other values in their place, can miss the bound.
Values may be sent and summed in bfloat16 or wider, within the bound.
No kernel may reach another device: no remote copies, remote signals or barrier semaphores. Data moves between devices by JAX's collectives and lax.ppermute only.
A program may use at most 128 MiB of HBM per device.

v0:
```python
import math

import jax
import jax.numpy as jnp
from jax import lax
from jax.sharding import PartitionSpec as P

HEAD_DIM = 128
CAP = 2


rope_base = 500000.0


def rotate(values, positions):
    half_dim = values.shape[-1] // 2
    frequency = jnp.exp(
        jnp.arange(half_dim, dtype=jnp.float32) * (-2.0 * math.log(rope_base) / values.shape[-1])
    )
    angles = positions.astype(jnp.float32)[:, None] * frequency[None, :]
    cosine = jnp.cos(angles)[:, None, :]
    sine_part = jnp.sin(angles)[:, None, :]
    lower_half = values[..., :half_dim]
    upper_half = values[..., half_dim:]
    return jnp.concatenate(
        [
            lower_half * cosine - upper_half * sine_part,
            upper_half * cosine + lower_half * sine_part,
        ],
        axis=-1,
    )


def attend(queries, new_key, new_value, cache, lengths):
    row_count = queries.shape[0]
    groups = new_key.shape[1]
    per_group = queries.shape[1] // groups
    head_dim = queries.shape[2]
    window = cache.shape[2]
    grouped = queries.reshape(row_count, groups, per_group, head_dim)
    cached_keys = cache[:, 0].reshape(row_count, window, groups, head_dim)
    cached_values = cache[:, 1].reshape(row_count, window, groups, head_dim)
    factor = 1.0 / math.sqrt(head_dim)
    scores = (
        jnp.einsum("rgqd,rlgd->rgql", grouped, cached_keys, preferred_element_type=jnp.float32)
        * factor
    )
    visible = jnp.arange(window)[None, :] < lengths[:, None]
    scores = jnp.where(visible[:, None, None, :], scores, -1e30)
    own_score = (
        jnp.einsum("rgqd,rgd->rgq", grouped, new_key, preferred_element_type=jnp.float32) * factor
    )
    highest = jnp.maximum(jnp.max(scores, axis=-1), own_score)
    old_terms = jnp.exp(scores - highest[..., None])
    newest = jnp.exp(own_score - highest)
    denominator = jnp.sum(old_terms, axis=-1) + newest
    old_weights = (old_terms / denominator[..., None]).astype(jnp.bfloat16)
    new_weight = (newest / denominator).astype(jnp.bfloat16)
    combined = jnp.einsum(
        "rgql,rlgd->rgqd", old_weights, cached_values, preferred_element_type=jnp.float32
    )
    combined = (
        combined
        + new_weight.astype(jnp.float32)[..., None] * new_value.astype(jnp.float32)[:, :, None, :]
    )
    return combined.reshape(row_count, groups * per_group * head_dim).astype(jnp.bfloat16)


def lookup_slots(row_ids, placement):
    adapters = placement.shape[0]
    matching = row_ids[:, None] == jnp.arange(adapters, dtype=jnp.int32)[None, :]
    return jnp.sum(jnp.where(matching, placement[None, :], 0), axis=1)


def route_rows(attended, slot_of, routed, capacity, adapter_down):
    owners = lax.axis_size("gx")
    local_slots = adapter_down.shape[0]
    adapters = owners * local_slots
    row_count = attended.shape[0]
    matching = (slot_of[:, None] == slot_of[None, :]) & routed[:, None] & routed[None, :]
    earlier = jnp.arange(row_count)[:, None] > jnp.arange(row_count)[None, :]
    arrival = jnp.sum((matching & earlier).astype(jnp.int32), axis=1)
    target = slot_of * capacity + arrival
    placed = jnp.arange(adapters * capacity, dtype=jnp.int32)[:, None] == target[None, :]
    placed = placed & (routed & (arrival < capacity))[None, :]
    dispatch = placed.astype(jnp.bfloat16)
    outgoing = jnp.dot(dispatch, attended, preferred_element_type=jnp.float32).astype(jnp.bfloat16)
    outgoing = outgoing.reshape(adapters, capacity, attended.shape[1])
    incoming = lax.all_to_all(outgoing, "gx", split_axis=0, concat_axis=0, tiled=True)
    slot_count = incoming.shape[1]
    grouped = incoming.reshape(owners, local_slots, slot_count, incoming.shape[2])
    partial_rank = jnp.einsum(
        "nskh,srh->nskr", grouped, adapter_down, preferred_element_type=jnp.float32
    )
    partial_rank = partial_rank.reshape(adapters, slot_count, partial_rank.shape[3])
    returned = lax.all_to_all(partial_rank, "gx", split_axis=0, concat_axis=0, tiled=True)
    returned = returned.reshape(adapters * capacity, returned.shape[2])
    return jnp.dot(dispatch.T.astype(jnp.float32), returned, precision=lax.Precision.HIGHEST)


def on_device(
    states,
    w_query,
    w_key_value,
    w_out,
    cache_kv,
    lengths,
    adapter_ids,
    placement,
    adapter_down,
    up_weight_slots,
):
    local_rows = cache_kv.shape[0]
    query_width = w_query.shape[1]
    pair_width = w_key_value.shape[1] * w_key_value.shape[2]
    flat_pairs = w_key_value.reshape(w_key_value.shape[0], pair_width)
    projected = lax.psum_scatter(
        jnp.concatenate(
            [
                jnp.dot(states, w_query, preferred_element_type=jnp.float32),
                jnp.dot(states, flat_pairs, preferred_element_type=jnp.float32),
            ],
            axis=1,
        ),
        "gx",
        scatter_dimension=0,
        tiled=True,
    )
    queries = rotate(
        projected[:, :query_width].reshape(local_rows, query_width // HEAD_DIM, HEAD_DIM), lengths
    )
    queries = queries.astype(jnp.bfloat16)
    key_value = projected[:, query_width:].reshape(
        local_rows, 2, pair_width // (2 * HEAD_DIM), HEAD_DIM
    )
    new_key = rotate(key_value[:, 0], lengths).astype(jnp.bfloat16)
    new_value = key_value[:, 1].astype(jnp.bfloat16)
    attended = attend(queries, new_key, new_value, cache_kv, lengths)
    adapters = placement.shape[0]
    block_start = lax.axis_index("gx") * local_rows
    my_ids = lax.dynamic_slice_in_dim(adapter_ids, block_start, local_rows, 0)
    slot_of = lookup_slots(my_ids, placement)
    partial_rank = route_rows(
        attended, slot_of, jnp.ones((local_rows,), jnp.bool_), CAP, adapter_down
    )
    owners = lax.axis_size("gx")
    halves = lax.axis_size("gy")
    gathered = lax.all_gather(partial_rank[None], ("gx", "gy"), axis=0, tiled=True)
    full_rank = jnp.sum(gathered.reshape(owners, halves, local_rows, gathered.shape[2]), axis=1)
    full_rank = full_rank.reshape(owners * local_rows, gathered.shape[2])
    half_rows = owners * local_rows // halves
    start_row = lax.axis_index("gy") * half_rows
    my_rank = lax.dynamic_slice_in_dim(full_rank, start_row, half_rows, 0).astype(jnp.bfloat16)
    half_slots = lookup_slots(
        lax.dynamic_slice_in_dim(adapter_ids, start_row, half_rows, 0), placement
    )
    chosen = half_slots[:, None] == jnp.arange(adapters, dtype=jnp.int32)[None, :]
    spread_rows = jnp.where(chosen[:, :, None], my_rank[:, None, :], jnp.zeros((), jnp.bfloat16))
    spread_rows = spread_rows.reshape(half_rows, adapters * my_rank.shape[1])
    adapter_update = jnp.dot(
        spread_rows,
        up_weight_slots.reshape(adapters * up_weight_slots.shape[1], up_weight_slots.shape[2]),
        preferred_element_type=jnp.float32,
    )
    partial_out = jnp.dot(
        lax.all_gather(attended, "gx", axis=0, tiled=True),
        w_out,
        preferred_element_type=jnp.float32,
    )
    base_output = lax.psum_scatter(partial_out, "gy", scatter_dimension=0, tiled=True)
    return (base_output + adapter_update).astype(jnp.bfloat16)


def solution(mesh):
    return jax.shard_map(
        on_device,
        mesh=mesh,
        in_specs=(
            P("groups", "gx"),
            P("gx", "gy"),
            P("gx", None, "gy"),
            P("gy", "gx"),
            P(("groups", "gx"), None, None, "gy"),
            P(("groups", "gx")),
            P("groups"),
            P(),
            P("gx", None, "gy"),
            P(None, None, "gx"),
        ),
        out_specs=P(("groups", "gy"), "gx"),
        check_vma=False,
    )
```

profile of v0, /device:TPU:0, one launch (start us, length us, event | category | flops | bytes accessed | tf_op | source)
XLA Modules:
  0.0 208.0 jit_solution(375637549725639729)
XLA Ops:
  6.5 2.3 %copy.58 = bf16[128,8,2,512]{3,1,2,0:T(8,128)(2,1)S(1)} copy(bf16[128,8,2,512]{3,2,1,0:T(2,128)(2,1)} %bitcast.62) | data formatting | bytes 4194304
  8.9 0.6 fusion.40
  9.5 5.2 %fusion.39 = f32[192,4096]{1,0:T(8,128)S(1)} fusion(bf16[192,1024]{1,0:T(8,128)(2,1)S(1)} %copy-done.3, bf16[1024,4096]{1,0:T(8,128)(2,1)} %param.11), kind=kOutput, calls=%fused_computation.70 | convolution fusion | flops 1610612736 | bytes 11927552 | tf_op jit(solution)/shard_map/dot_general | solution.py:120
  14.7 2.3 %pad_maximum_fusion = f32[192,5120]{1,0:T(8,128)} fusion(f32[192,1024]{1,0:T(8,128)S(1)} %fusion.40, f32[192,4096]{1,0:T(8,128)S(1)} %fusion.39), kind=kLoop, calls=%fused_computation.1 | loop fusion | flops 983040 | bytes 7864320 | tf_op jit(solution)/shard_map/concatenate | solution.py:118
  17.0 0.6 copy-done.4
  17.6 6.2 %fusion.37 = (bf16[24,1,128,512]{3,2,1,0:T(8,128)(2,1)}, bf16[24,1,128,512]{3,2,1,0:T(8,128)(2,1)}) fusion(bf16[24,2,128,512]{3,2,1,0:T(8,128)(2,1)} %param.14), kind=kLoop, calls=%fused_computation.68 | loop fusion | bytes 12582912 | tf_op jit(solution)/shard_map/slice | solution.py:41
  23.8 4.8 %copy.55 = bf16[24,1,128,512]{2,3,0,1:T(8,128)(2,1)} copy(bf16[24,1,128,512]{3,2,1,0:T(8,128)(2,1)} %get-tuple-element.5) | data formatting | bytes 6291456
  28.6 4.6 %copy.56 = bf16[24,1,128,512]{2,3,0,1:T(8,128)(2,1)} copy(bf16[24,1,128,512]{3,2,1,0:T(8,128)(2,1)} %get-tuple-element.6) | data formatting | bytes 6291456
  33.5 71.0 %reduce-scatter.3.cloned.1.call-done = f32[24,5120]{1,0:T(8,128)} async-done(((f32[192,5120]{1,0:T(8,128)}), f32[24,5120]{1,0:T(8,128)}) %reduce-scatter.3.cloned.1.call-update) | async-done | bytes 491536 | tf_op jit(solution)/shard_map/reduce_scatter | solution.py:117
  104.5 0.9 slice.44
  105.5 1.2 slice_bitcast_fusion
  106.8 0.2 fusion.15
  107.2 0.3 fusion.19
  107.5 1.1 fusion.38
  108.6 0.4 fusion.12
  109.1 1.8 fusion.4
  110.8 0.8 copy.67
  111.9 0.2 convert_reduce_fusion
  112.1 0.3 convolution_convert_fusion
  112.4 1.1 reshape.154
  113.6 4.3 %all-to-all-start = ((bf16[32,2,4096]{2,1,0:T(2,128)(2,1)}), bf16[32,2,4096]{2,1,0:T(2,128)(2,1)S(1)}, u32[]{:S(2)}, u32[]{:S(2)}) async-start(bf16[32,2,4096]{2,1,0:T(2,128)(2,1)} %reshape.154), calls=%async_computation.2 | async-start | bytes 1048576 | tf_op jit(solution)/shard_map/all_to_all | solution.py:89
  117.9 41.8 %all-gather.3.cloned.1.call-done = bf16[192,4096]{1,0:T(8,128)(2,1)} async-done(((bf16[24,4096]{1,0:T(8,128)(2,1)}), bf16[192,4096]{1,0:T(8,128)(2,1)}) %all-gather.3.cloned.1.call-update) | async-done | bytes 1572880 | tf_op jit(solution)/shard_map/all_gather | solution.py:166
  159.6 6.6 %fusion.41 = f32[192,1024]{1,0:T(8,128)} fusion(bf16[192,4096]{1,0:T(8,128)(2,1)} %all-gather.3.cloned.1.call-done, bf16[4096,1024]{1,0:T(8,128)(2,1)} %param.13), kind=kOutput, calls=%fused_computation.72 | convolution fusion | flops 1610612736 | bytes 10747904 | tf_op jit(solution)/shard_map/dot_general | solution.py:165
  166.4 0.7 fusion.6
  167.1 0.7 reshape.167
  167.8 3.4 %all-to-all-start.1 = ((f32[8,1,512]{2,1,0:T(1,128)}), f32[8,1,512]{2,1,0:T(1,128)S(1)}, u32[]{:S(2)}, u32[]{:S(2)}) async-start(f32[8,1,512]{2,1,0:T(1,128)} %reshape.167), calls=%async_computation.3 | async-start | bytes 32768 | tf_op jit(solution)/shard_map/all_to_all | solution.py:96
  171.3 6.6 %all-to-all-done.1 = f32[8,1,512]{2,1,0:T(1,128)S(1)} async-done(((f32[8,1,512]{2,1,0:T(1,128)}), f32[8,1,512]{2,1,0:T(1,128)S(1)}, u32[]{:S(2)}, u32[]{:S(2)}) %all-to-all-start.1) | async-done | bytes 16416 | tf_op jit(solution)/shard_map/all_to_all | solution.py:96
  177.8 0.5 broadcast.83
  178.3 0.7 reduce
  179.1 0.2 fusion.22
  179.3 18.2 %all-gather = f32[384,64]{1,0:T(8,128)S(1)} all-gather(f32[24,64]{1,0:T(8,128)S(1)} %fusion.22), channel_id=2, replica_groups=mesh['groups'=2,'gx'=8,'gy'=2] {'gx','gy'}, dimensions={0}, use_global_device_ids=true | all-gather | bytes 104448 | tf_op jit(solution)/shard_map/all_gather | solution.py:148
  197.7 3.8 %fusion.5 = bf16[96,1024]{1,0:T(8,128)(2,1)} fusion(f32[96,1024]{1,0:T(8,128)} %reduce-scatter.5.cloned.1.call-done, bf16[32,64,1024]{2,1,0:T(8,128)(2,1)} %param.19, pred[96,32]{0,1:T(8,128)(4,1)S(1)} %iota_compare_fusion.1, bf16[96,64]{0,1:T(8,128)(2,1)S(1)} %copy.57), kind=kOutput, calls=%fused_computation.10 | convolution fusion | flops 403046400 | bytes 4799488 | tf_op jit(solution)/shard_map/dot_general | solution.py:160
  (46 shorter events, 1.5 us)
Async XLA Ops:
  6.5 159.9 %copy-start = (bf16[4,64,4096]{2,1,0:T(8,128)(2,1)S(1)}, bf16[4,64,4096]{2,1,0:T(8,128)(2,1)}, u32[]{:S(2)}) copy-start(bf16[4,64,4096]{2,1,0:T(8,128)(2,1)} %param.18) | copy-start | bytes 6291460
  6.5 2.3 %copy-start.3 = (bf16[192,1024]{1,0:T(8,128)(2,1)S(1)}, bf16[192,1024]{1,0:T(8,128)(2,1)}, u32[]{:S(2)}) copy-start(bf16[192,1024]{1,0:T(8,128)(2,1)} %param.10) | copy-start | bytes 1179652
  6.5 98.0 %reduce-scatter.3.cloned.1.call-start = ((), (), s32[]{:S(2)}) async-start(), calls=%async_computation.4 | async-start | bytes 4423680 | tf_op jit(solution)/shard_map/reduce_scatter | solution.py:117
  16.9 0.7 copy-start.4
  16.9 142.7 %all-gather.3.cloned.1.call-start = ((), (), s32[]{:S(2)}) async-start(), calls=%async_computation.5 | async-start | bytes 1769472 | tf_op jit(solution)/shard_map/all_gather | solution.py:166
  105.5 2.0 copy-start.1
  107.0 2.1 %copy-start.2 = (bf16[24,1,128,512]{2,3,0,1:T(8,128)(2,1)S(1)}, bf16[24,1,128,512]{2,3,0,1:T(8,128)(2,1)}, u32[]{:S(2)}) copy-start(bf16[24,1,128,512]{2,3,0,1:T(8,128)(2,1)} %copy.56) | copy-start | bytes 9437188
  109.0 2.7 %copy-start.5 = (s32[192]{0:T(256)S(1)}, s32[192]{0:T(256)}, u32[]{:S(2)}) copy-start(s32[192]{0:T(256)} %param.16) | copy-start | bytes 2308
  109.0 2.7 %copy-start.6 = (s32[32]{0:T(128)S(1)}, s32[32]{0:T(128)}, u32[]{:S(2)}) copy-start(s32[32]{0:T(128)} %param.17) | copy-start | bytes 388
  113.6 52.8 %all-to-all-start = ((bf16[32,2,4096]{2,1,0:T(2,128)(2,1)}), bf16[32,2,4096]{2,1,0:T(2,128)(2,1)S(1)}, u32[]{:S(2)}, u32[]{:S(2)}) async-start(bf16[32,2,4096]{2,1,0:T(2,128)(2,1)} %reshape.154), calls=%async_computation.2 | async-start | bytes 1048576 | tf_op jit(solution)/shard_map/all_to_all | solution.py:89
  117.8 79.9 %reduce-scatter.5.cloned.1.call-start = ((), (), s32[]{:S(2)}) async-start(), calls=%async_computation.6 | async-start | bytes 1179648 | tf_op jit(solution)/shard_map/reduce_scatter | solution.py:170
  167.8 10.0 %all-to-all-start.1 = ((f32[8,1,512]{2,1,0:T(1,128)}), f32[8,1,512]{2,1,0:T(1,128)S(1)}, u32[]{:S(2)}, u32[]{:S(2)}) async-start(f32[8,1,512]{2,1,0:T(1,128)} %reshape.167), calls=%async_computation.3 | async-start | bytes 32768 | tf_op jit(solution)/shard_map/all_to_all | solution.py:96
Sparse Core Ops, SparseCore 0:
  17.1 87.4 reduce-scatter.2
  111.8 47.8 all-gather.2
  166.3 7.0 reduce-scatter.4
where the time goes:
time: 209 us; the launch traced here: 208 us
  waiting for transfers between devices  119 us (57%)
  local copies, waits for them, and re-layouts  24.3 us (12%)
  matrix products  20.4 us (10%)
  blocking collectives  18.2 us (9%)
  between operations  13.4 us (6%)
  starting transfers between devices  7.75 us (4%)
  other arithmetic  4.47 us (2%)
    reduce_scatter x1, waiting for transfers between devices, on_device(): lax.psum_scatter(jnp.concatenate([jnp.dot(states, w_query, preferred_elem...  71 us
    all_gather x1, waiting for transfers between devices, on_device(): lax.all_gather(attended, 'gx', axis=0, tiled=True)  41.8 us
    all_gather x1, blocking collectives, on_device(): lax.all_gather(partial_rank[None], ('gx', 'gy'), axis=0, tiled=True)  18.2 us
    unnamed x23, local copies, waits for them, and re-layouts  15.3 us
    all_to_all x1, waiting for transfers between devices, route_rows(): lax.all_to_all(partial_rank, 'gx', split_axis=0, concat_axis=0, tiled=True)  6.57 us
    dot_general x1, matrix products, on_device(): jnp.dot(lax.all_gather(attended, 'gx', axis=0, tiled=True), w_out, prefer...  6.55 us
    slice x1, local copies, waits for them, and re-layouts, attend(): cached_keys = cache[:, 0].reshape(row_count, window, groups, head_dim)  6.22 us
    dot_general x1, matrix products, on_device(): jnp.dot(states, w_query, preferred_element_type=jnp.float32)  5.18 us
  transfers between devices with their start and end apart: 5, of which 3 were waited for; matrix products, arithmetic and copies ran while one was open for 13% of the time, Pallas kernels for 0%

commit v1 on v0

v1 whole, which is shorter than its diff:
```python
import functools
import math

import jax
import jax.numpy as jnp
from jax import lax
from jax.experimental import pallas as pl
from jax.experimental.pallas import tpu as pltpu
from jax.sharding import PartitionSpec as P

HEAD_DIM = 128
CHUNKS = 2
PIN = True
SPLIT = True
STAGE = False
STAGE_UP = False

rope_base = 500000.0


def rotation(positions):
    half_dim = HEAD_DIM // 2
    frequency = jnp.exp(
        jnp.arange(half_dim, dtype=jnp.float32) * (-2.0 * math.log(rope_base) / HEAD_DIM)
    )
    angles = positions.astype(jnp.float32)[:, None] * frequency[None, :]
    cosine, sine_part = jnp.cos(angles), jnp.sin(angles)
    return jnp.concatenate([cosine, cosine, -sine_part, sine_part], axis=1)


def split_copies(source, target, sems, pieces):
    count = source.shape[0] // pieces
    return [
        pltpu.make_async_copy(
            source.at[pl.ds(n * count, count)], target.at[pl.ds(n * count, count)], sems.at[n]
        )
        for n in range(pieces)
    ]


def stage_kernel(pieces, in_ref, out_ref, sems):
    copies = split_copies(in_ref, out_ref, sems, pieces)
    for copy in copies:
        copy.start()
    for copy in copies:
        copy.wait()


def stage(x):
    pieces = math.gcd(8, x.shape[0])
    return pl.pallas_call(
        functools.partial(stage_kernel, pieces),
        in_specs=[pl.BlockSpec(memory_space=pl.ANY)],
        out_specs=pl.BlockSpec(memory_space=pltpu.VMEM),
        out_shape=jax.ShapeDtypeStruct(x.shape, x.dtype),
        scratch_shapes=[pltpu.SemaphoreType.DMA((pieces,))],
        compiler_params=pltpu.CompilerParams(vmem_limit_bytes=24 * 2**20),
        cost_estimate=pl.CostEstimate(flops=0, bytes_accessed=2 * x.nbytes, transcendentals=0),
        name="stage",
    )(x)


def project_kernel(
    bit, local_rows, start, tile, side_ref, states_hbm, weight_hbm, away_ref, kept_ref,
    states_s, weight_s, sems,
):
    width, columns = weight_s.shape
    pieces = sems.shape[0] - 1
    depth = width // pieces
    copies = [pltpu.make_async_copy(states_hbm, states_s, sems.at[pieces])]
    for n in range(pieces):
        at = pl.ds(n * depth, depth)
        copies.append(
            pltpu.make_async_copy(
                weight_hbm.at[at, pl.ds(start, columns)], weight_s.at[at], sems.at[n]
            )
        )
    for copy in copies:
        copy.start()
    for copy in copies:
        copy.wait()
    even = side_ref[0] == 0
    for n in range(columns // tile):
        at = slice(n * tile, (n + 1) * tile)
        part = jnp.dot(states_s[...], weight_s[:, at], preferred_element_type=jnp.float32)
        sides = [
            jnp.concatenate(
                [
                    part[block * local_rows : (block + 1) * local_rows]
                    for block in range(part.shape[0] // local_rows)
                    if (block >> bit) % 2 == which
                ],
                axis=0,
            )
            for which in range(2)
        ]
        away_ref[:, at] = jnp.where(even, sides[1], sides[0]).astype(jnp.bfloat16)
        kept_ref[:, at] = jnp.where(even, sides[0], sides[1])


def project(side, states, weight, start, columns, bit, local_rows):
    rows, width = states.shape
    tile = math.gcd(512, columns)
    kept_rows = rows // 2
    pieces = math.gcd(8, width // 16)
    vmem = pl.BlockSpec(memory_space=pltpu.VMEM)
    hbm = pl.BlockSpec(memory_space=pl.ANY)
    return pl.pallas_call(
        functools.partial(project_kernel, bit, local_rows, start, tile),
        in_specs=[pl.BlockSpec(memory_space=pltpu.SMEM), hbm, hbm],
        out_specs=[vmem, vmem],
        out_shape=[
            jax.ShapeDtypeStruct((kept_rows, columns), jnp.bfloat16),
            jax.ShapeDtypeStruct((kept_rows, columns), jnp.float32),
        ],
        scratch_shapes=[
            pltpu.VMEM((rows, width), states.dtype),
            pltpu.VMEM((width, columns), weight.dtype),
            pltpu.SemaphoreType.DMA((pieces + 1,)),
        ],
        compiler_params=pltpu.CompilerParams(vmem_limit_bytes=58 * 2**20),
        cost_estimate=pl.CostEstimate(
            flops=2 * rows * width * columns,
            bytes_accessed=2 * width * (rows + columns) + 6 * kept_rows * columns,
            transcendentals=0,
        ),
        name="project",
    )(side, states, weight)


def attend_kernel(heads, groups, far, offsets, lengths_ref, trig_ref, *refs):
    q_refs = refs[: far + 1]
    kv_refs = refs[far + 1 : 2 * far + 2]
    cache_s, out_ref, q_s, k_s, v_s, o_s = refs[2 * far + 2 :]
    per_group = heads // groups
    q_start, key_start, value_start = offsets
    rows, _, window, columns = cache_s.shape

    cosine = trig_ref[:, :HEAD_DIM]
    signed = trig_ref[:, HEAD_DIM:]

    def total(parts, start):
        value = parts[0][:, start : start + HEAD_DIM]
        for ref in parts[1:]:
            value = value + ref[:, start : start + HEAD_DIM].astype(jnp.float32)
        return value

    def turned(value):
        value = value * cosine + pltpu.roll(value, HEAD_DIM // 2, 1) * signed
        return value.astype(jnp.bfloat16).astype(jnp.float32)

    q_s[...] = jnp.zeros_like(q_s)
    for g in range(groups):
        key = turned(total(kv_refs, key_start + g * HEAD_DIM))
        value = total(kv_refs, value_start + g * HEAD_DIM)
        value = value.astype(jnp.bfloat16).astype(jnp.float32)
        for j in range(g * per_group, (g + 1) * per_group):
            q_s[:, j, g * HEAD_DIM : (g + 1) * HEAD_DIM] = turned(
                total(q_refs, q_start + j * HEAD_DIM)
            )
            k_s[:, j, :] = key
            v_s[:, j, :] = value

    factor = 1.0 / math.sqrt(HEAD_DIM)
    slot = lax.broadcasted_iota(jnp.int32, (heads, window), 1)
    q = q_s[...]
    flat = q[:, :, :HEAD_DIM]
    for g in range(1, groups):
        flat = flat + q[:, :, g * HEAD_DIM : (g + 1) * HEAD_DIM]
    own = jnp.sum(flat * k_s[...], axis=2, keepdims=True) * factor
    low = q.astype(jnp.bfloat16)
    scores = []
    for r in range(rows):
        score = lax.dot_general(
            low[r],
            cache_s[r, 0],
            (((1,), (1,)), ((), ())),
            preferred_element_type=jnp.float32,
        )
        scores.append(jnp.where(slot < lengths_ref[r], score * factor, -1e30))
    scores = jnp.stack(scores, axis=0)
    highest = jnp.maximum(jnp.max(scores, axis=2, keepdims=True), own)
    old_terms = jnp.exp(scores - highest)
    newest = jnp.exp(own - highest)
    denominator = jnp.sum(old_terms, axis=2, keepdims=True) + newest
    old_weights = (old_terms / denominator).astype(jnp.bfloat16)
    new_weight = (newest / denominator).astype(jnp.bfloat16).astype(jnp.float32)
    added = new_weight * v_s[...]
    for r in range(rows):
        mixed = jnp.dot(old_weights[r], cache_s[r, 1], preferred_element_type=jnp.float32)
        mixed = jnp.concatenate(
            [
                mixed[g * per_group : (g + 1) * per_group, g * HEAD_DIM : (g + 1) * HEAD_DIM]
                for g in range(groups)
            ],
            axis=0,
        )
        o_s[r] = mixed + added[r]
    for j in range(heads):
        out_ref[:, j * HEAD_DIM : (j + 1) * HEAD_DIM] = o_s[:, j, :].astype(jnp.bfloat16)


def attend(chunk, heads, groups, offsets, lengths, trig, q_parts, kv_parts, cache):
    rows, _, window, _ = cache.shape

    def whole(x):
        return pl.BlockSpec(x.shape, lambda i, s: (0,) * x.ndim)

    far = len(q_parts) - 1
    small = [trig, *q_parts, *kv_parts]
    return pl.pallas_call(
        functools.partial(attend_kernel, heads, groups, far, offsets),
        grid_spec=pltpu.PrefetchScalarGridSpec(
            num_scalar_prefetch=1,
            grid=(1,),
            in_specs=[whole(x) for x in small]
            + [
                pl.BlockSpec(
                    (rows, 2, window, groups * HEAD_DIM), lambda i, s: (0, 0, 0, chunk)
                )
            ],
            out_specs=pl.BlockSpec((rows, heads * HEAD_DIM), lambda i, s: (0, 0)),
            scratch_shapes=[
                pltpu.VMEM((rows, heads, groups * HEAD_DIM), jnp.float32),
                pltpu.VMEM((rows, heads, HEAD_DIM), jnp.float32),
                pltpu.VMEM((rows, heads, HEAD_DIM), jnp.float32),
                pltpu.VMEM((rows, heads, HEAD_DIM), jnp.float32),
            ],
        ),
        out_shape=jax.ShapeDtypeStruct((rows, heads * HEAD_DIM), jnp.bfloat16),
        compiler_params=pltpu.CompilerParams(vmem_limit_bytes=24 * 2**20),
        cost_estimate=pl.CostEstimate(
            flops=4 * rows * heads * window * HEAD_DIM * groups,
            bytes_accessed=4 * rows * window * groups * HEAD_DIM,
            transcendentals=rows * heads * window,
        ),
        name="attend",
    )(lengths, *small, cache)


def finish_kernel(
    local_rows, place_ref, slots_ref, low_ref, kept_ref, sent_ref, up_ref, out_ref, placed
):
    rows, rank = low_ref.shape
    depth = up_ref.shape[0]
    wide = math.gcd(256, depth)
    blocks = rows // (2 * local_rows)
    for which in range(2):
        for line in range(blocks):
            start = (which * blocks + line) * local_rows
            at = slice(start, start + local_rows)
            target = 2 * (line ^ place_ref[1]) + (which ^ place_ref[0])
            target = pl.multiple_of(target * local_rows, 8)
            placed[pl.ds(target, local_rows), :] = kept_ref[at, :] + sent_ref[at, :]
    low = jnp.concatenate([low_ref[...].astype(jnp.float32)] * (wide // rank), axis=1)
    offset = slots_ref[...] - lax.broadcasted_iota(jnp.int32, (rows, wide), 1) // rank
    total = placed[...]
    for start in range(0, depth, wide):
        spread = jnp.where(offset == start // rank, low, 0.0).astype(jnp.bfloat16)
        total = total + jnp.dot(
            spread, up_ref[start : start + wide, :], preferred_element_type=jnp.float32
        )
    out_ref[...] = total.astype(jnp.bfloat16)


def finish(local_rows, place, slots, low_rank, kept, sent, up):
    rows, columns = kept.shape
    vmem = pl.BlockSpec(memory_space=pltpu.VMEM)
    return pl.pallas_call(
        functools.partial(finish_kernel, local_rows),
        in_specs=[pl.BlockSpec(memory_space=pltpu.SMEM)] + [vmem] * 5,
        out_specs=vmem,
        out_shape=jax.ShapeDtypeStruct((rows, columns), jnp.bfloat16),
        scratch_shapes=[pltpu.VMEM((rows, columns), jnp.float32)],
        compiler_params=pltpu.CompilerParams(vmem_limit_bytes=24 * 2**20),
        cost_estimate=pl.CostEstimate(
            flops=2 * rows * up.shape[0] * columns,
            bytes_accessed=2 * up.shape[0] * columns,
            transcendentals=0,
        ),
        name="finish",
    )(place, slots, low_rank, kept, sent, up)


def lookup_slots(row_ids, placement):
    adapters = placement.shape[0]
    matching = row_ids[:, None] == jnp.arange(adapters, dtype=jnp.int32)[None, :]
    return jnp.sum(jnp.where(matching, placement[None, :], 0), axis=1)


def on_device(
    states,
    w_query,
    w_key_value,
    w_out,
    cache_kv,
    lengths,
    adapter_ids,
    placement,
    adapter_down,
    up_weight_slots,
):
    owners = lax.axis_size("gx")
    lines = owners // 2
    local_rows = cache_kv.shape[0]
    side_rows = lines * local_rows
    half_rows = side_rows // 2
    me = lax.axis_index("gx")
    half = lax.axis_index("gy")
    my_line, my_side = me // 2, me % 2
    line_bits = [1 << n for n in range(lines.bit_length() - 1)]

    def my_bit(bit):
        return (my_line // bit) % 2

    def swap(x, bit):
        return lax.ppermute(x, "gx", [(i, i ^ bit) for i in range(owners)])

    def swap_half(x):
        return lax.ppermute(x, "gy", [(0, 1), (1, 0)])

    q_cols = w_query.shape[1] // CHUNKS
    kv_cols = w_key_value.shape[2]
    side = my_side.astype(jnp.int32).reshape(1)
    trig = rotation(lengths)
    pair = w_key_value.reshape(w_key_value.shape[0], 2 * kv_cols)

    bits = list(range(owners.bit_length() - 1))

    def bit_of(bit):
        return (me >> bit) % 2

    def projected(states, weight, start, columns, bit):
        mine = bit_of(bit).astype(jnp.int32).reshape(1)
        away, kept = project(mine, states, weight, start, columns, bit, local_rows)
        away, kept, states = lax.optimization_barrier((away, kept, states))
        return (kept, swap(away, 1 << bit)), states

    side_first, line_first = bits, bits[1:] + bits[:1]
    first, states = projected(states, w_query, 0, q_cols, side_first[0])
    second, states = projected(states, w_query, q_cols, q_cols, line_first[0])
    pairs, states = projected(states, pair, 0, 2 * kv_cols, side_first[0])
    sums = [first, second, pairs]
    orders = [side_first, line_first, side_first]
    left = [[bit for bit in bits if bit != order[0]] for order in orders]
    before = None
    for n, at in [(n, at) for at in range(1, len(bits)) for n in ((0, 1, 2) if at == 1 else (0, 2, 1))]:
        kept, got = sums[n]
        if before is not None:
            got, _ = lax.optimization_barrier((got, before))
        before = got
        bit, columns = orders[n][at], kept.shape[1]
        inner = (1 << left[n].index(bit)) * local_rows
        left[n].remove(bit)
        total = (kept + got.astype(jnp.float32)).reshape(-1, 2, inner, columns)
        away = lax.dynamic_index_in_dim(total, 1 - bit_of(bit), 1, keepdims=False)
        home = lax.dynamic_index_in_dim(total, bit_of(bit), 1, keepdims=False)
        away = away.reshape(-1, columns).astype(jnp.bfloat16)
        if PIN:
            before = (before, away)
        sums[n] = (home.reshape(-1, columns), swap(away, 1 << bit))
    q_sums, (kv_sums, kv_at) = sums[:2], (sums[2], 0)

    groups = kv_cols // HEAD_DIM // CHUNKS
    attended = []
    for c in range(CHUNKS):
        key_at = kv_at + c * groups * HEAD_DIM
        if c:
            far, _ = lax.optimization_barrier((q_sums[c][-1], attended[-1]))
            q_sums[c] = (*q_sums[c][:-1], far)
        attended.append(
            attend(
                c,
                q_cols // HEAD_DIM,
                groups,
                (0, key_at, key_at + kv_cols),
                lengths,
                trig,
                q_sums[c],
                kv_sums,
                cache_kv,
            )
        )

    local_slots = adapter_down.shape[0]
    rank = adapter_down.shape[1]
    down = adapter_down.reshape(local_slots * rank, adapter_down.shape[2])

    def product(x, weight, axis, c):
        at = c * q_cols
        return lax.dot_general(
            x[:, at : at + q_cols],
            lax.slice_in_dim(weight, at, at + q_cols, axis=axis),
            (((1,), (axis,)), ((), ())),
            preferred_element_type=jnp.float32,
        )

    def summed(x, weight, axis):
        return sum(product(x, weight, axis, c) for c in range(CHUNKS))

    own = jnp.concatenate(attended, axis=1)
    far = lines // 2
    blocks = [own, *(swap(own, 2 << n) for n in range(len(line_bits)))]
    blocks = {0: own, **{bit: x for bit, x in zip(line_bits, blocks[1:])}}
    crossing = [swap(own, 1)]
    for k in range(1, far):
        if k not in blocks:
            blocks[k] = swap(blocks[k & (k - 1)], 2 * (k & -k))
    early = jnp.concatenate([blocks[k] for k in range(far)] + crossing, axis=0)
    out_early, shrunk_early = summed(early, w_out, 0), summed(early, down, 1)
    blocks[far], out_early, shrunk_early = lax.optimization_barrier(
        (blocks[far], out_early, shrunk_early)
    )
    for k in range(far + 1, lines):
        blocks[k] = swap(blocks[k & (k - 1)], 2 * (k & -k))
    blocks = [blocks[k] for k in range(lines)]
    crossing += [swap(x, 1) for x in blocks[1:]]
    late = jnp.concatenate(blocks[far:] + crossing[1:], axis=0)
    shrunk_late = summed(late, down, 1)
    up = up_weight_slots.reshape(-1, up_weight_slots.shape[2])

    def by_side(early, late):
        return [
            jnp.concatenate([early[:half_rows], late[:half_rows]], axis=0),
            jnp.concatenate([early[half_rows:], late[half_rows:]], axis=0),
        ]

    shrunk = by_side(shrunk_early, shrunk_late)

    slots = lookup_slots(adapter_ids, placement)
    here = slots[:, None] == me * local_slots + jnp.arange(local_slots)[None, :]
    x = jnp.stack(shrunk, axis=0).reshape(
        (2, 2) + (2,) * (len(line_bits) - 1) + (local_rows, local_slots, rank)
    )
    places = [my_side] + [my_bit(bit) for bit in reversed(line_bits)]
    for axis, place in enumerate(places):
        x = jnp.where(place == 0, x, jnp.flip(x, axis))
    x = jnp.moveaxis(x, 0, len(line_bits)).reshape(-1, local_slots, rank)
    x = jnp.sum(jnp.where(here[:, :, None], x, jnp.zeros(())), axis=1)

    def part(x, which):
        return lax.dynamic_slice_in_dim(x, which * side_rows, side_rows, 0)

    low_rank = (part(x, half) + swap_half(part(x, 1 - half))).astype(jnp.bfloat16)
    turns = [late] * CHUNKS
    turns[0], low_rank = lax.optimization_barrier((late, low_rank))
    low_rank = low_rank + swap(low_rank, 1)
    if SPLIT:
        turns[-1], low_rank = lax.optimization_barrier((late, low_rank))
    else:
        turns[-1] = turns[0]
    for x in [swap(low_rank, 2 * k) for k in range(1, lines)]:
        low_rank = low_rank + x

    out_late = sum(
        lax.optimization_barrier(product(turns[c], w_out, 0, c)) for c in range(CHUNKS)
    )
    same = my_bit(line_bits[-1]) == half
    outs = by_side(out_early, out_late)
    halves = [(x[:half_rows], x[half_rows:]) for x in outs]
    home = jnp.concatenate([jnp.where(same, *x) for x in halves], axis=0)
    away = jnp.concatenate([jnp.where(same, *x[::-1]) for x in halves], axis=0)
    place = jnp.stack([my_side, my_line % max(lines // 2, 1)]).astype(jnp.int32)
    return finish(
        local_rows,
        place,
        part(slots, half)[:, None],
        low_rank,
        home,
        swap_half(away),
        up,
    )


def solution(mesh):
    return jax.shard_map(
        on_device,
        mesh=mesh,
        in_specs=(
            P("groups", "gx"),
            P("gx", "gy"),
            P("gx", None, "gy"),
            P("gy", "gx"),
            P(("groups", "gx"), None, None, "gy"),
            P(("groups", "gx")),
            P("groups"),
            P(),
            P("gx", None, "gy"),
            P(None, None, "gx"),
        ),
        out_specs=P(("groups", "gy"), "gx"),
        check_vma=False,
    )
```

time: 209 us -> 94.7 us (0.45)
  waiting for transfers between devices: 119 us -> 26.5 us
  starting transfers between devices: 7.75 us -> 30.9 us
  local copies, waits for them, and re-layouts: 24.3 us -> 5.13 us
  blocking collectives: 18.2 us -> 0 us
  Pallas kernels: 0 us -> 17.6 us
  between operations: 13.4 us -> 0.81 us
  matrix products: 20.4 us -> 9.56 us
    reduce_scatter x2 -> x0, waiting for transfers between devices: 71.1 us -> none  [the longest x1 71 us: on_device(): lax.psum_scatter(jnp.concatenate([jnp.dot(states, w_query, preferred_elem...]
    all_gather x1 -> x0, waiting for transfers between devices: 41.8 us -> none  [on_device(): lax.all_gather(attended, 'gx', axis=0, tiled=True)]
    ppermute x0 -> x22, starting transfers between devices: none -> 30.9 us  [the longest x20 30.8 us: swap(): return lax.ppermute(x, 'gx', [(i, i ^ bit) for i in range(owners)])]
    ppermute x0 -> x22, waiting for transfers between devices: none -> 26.5 us  [the longest x20 25.4 us: swap(): return lax.ppermute(x, 'gx', [(i, i ^ bit) for i in range(owners)])]
    all_gather x1 -> x0, blocking collectives: 18.2 us -> none  [on_device(): lax.all_gather(partial_rank[None], ('gx', 'gy'), axis=0, tiled=True)]
    pallas_call x0 -> x6, Pallas kernels: none -> 17.6 us  [the longest x3 12.1 us: project(): pl.pallas_call(functools.partial(project_kernel, bit, local_rows, start,...]
    unnamed x23 -> x34, local copies, waits for them, and re-layouts: 15.3 us -> 4.25 us
    dot_general x10 -> x8, matrix products: 20.4 us -> 9.56 us  [product(): lax.dot_general(x[:, at:at + q_cols], lax.slice_in_dim(weight, at, at + q...]
  transfers between devices with their start and end apart: 5 -> 22, of which waited for: 3 -> 14; matrix products, arithmetic and copies ran while one was open for 13% -> 12% of each run, Pallas kernels for 0% -> 10%
where the time goes in v1:
time: 94.7 us; the launch traced here: 94.4 us
  starting transfers between devices  30.9 us (33%)
  waiting for transfers between devices  26.5 us (28%)
  Pallas kernels  17.6 us (19%)
  matrix products  9.56 us (10%)
  local copies, waits for them, and re-layouts  5.13 us (5%)
  other arithmetic  3.83 us (4%)
    ppermute x20, starting transfers between devices, swap(): return lax.ppermute(x, 'gx', [(i, i ^ bit) for i in range(owners)])  30.8 us
    ppermute x20, waiting for transfers between devices, swap(): return lax.ppermute(x, 'gx', [(i, i ^ bit) for i in range(owners)])  25.4 us
    pallas_call x3, Pallas kernels, project(): pl.pallas_call(functools.partial(project_kernel, bit, local_rows, start,...  12.1 us
    dot_general x8, matrix products, product(): lax.dot_general(x[:, at:at + q_cols], lax.slice_in_dim(weight, at, at + q...  9.56 us
    unnamed x34, local copies, waits for them, and re-layouts  4.25 us
    pallas_call x2, Pallas kernels, attend(): pl.pallas_call(functools.partial(attend_kernel, heads, groups, far, offse...  3.37 us
    add x6, other arithmetic, on_device(): total = (kept + got.astype(jnp.float32)).reshape(-1, 2, inner, columns)  2.53 us
    pallas_call x1, Pallas kernels, finish(): pl.pallas_call(functools.partial(finish_kernel, local_rows), in_specs=[pl...  2.09 us
  transfers between devices with their start and end apart: 22, of which 14 were waited for; matrix products, arithmetic and copies ran while one was open for 12% of the time, Pallas kernels for 10%

profile of v1, /device:TPU:0, one launch (start us, length us, event | category | flops | bytes accessed | tf_op | source)
XLA Modules:
  0.0 94.4 jit_solution(14597921179637413798)
XLA Ops:
  0.0 4.4 %project.3 = (bf16[96,2048]{1,0:T(8,128)(2,1)}, f32[96,2048]{1,0:T(8,128)}) custom-call(s32[1]{0:T(128)} %bitcast.3.side_ref, bf16[192,1024]{1,0:T(8,128)(2,1)} %states_hbm.3, bf16[1024,4096]{1,0:T(8,128)(2,1)} %weight_hbm.3), custom_call_target="tpu_custom_call" | custom-call | flops 805306368 | bytes 5767168 | tf_op jit(solution)/shard_map/project/pallas_call | solution.py:108
  4.4 3.0 %collective-permute-start = (bf16[96,2048]{1,0:T(8,128)(2,1)}, bf16[96,2048]{1,0:T(8,128)(2,1)}, u32[]{:S(2)}, u32[]{:S(2)}) collective-permute-start(bf16[96,2048]{1,0:T(8,128)(2,1)} %get-tuple-element.35), channel_id=1, source_target_pairs={{0,2},{2,0},{4,6},{6,4},{8,10},{10,8},{12,14},{14,12},{1,3},{3,1},... | collective-permute-start | bytes 1179656 | tf_op jit(solution)/shard_map/ppermute | solution.py:317
  7.4 4.5 %project.4 = (bf16[96,2048]{1,0:T(8,128)(2,1)}, f32[96,2048]{1,0:T(8,128)}) custom-call(s32[1]{0:T(128)} %bitcast.7.side_ref, bf16[192,1024]{1,0:T(8,128)(2,1)} %states_hbm.3, bf16[1024,4096]{1,0:T(8,128)(2,1)} %weight_hbm.3), custom_call_target="tpu_custom_call" | custom-call | flops 805306368 | bytes 5767168 | tf_op jit(solution)/shard_map/project/pallas_call | solution.py:108
  12.0 1.6 %collective-permute-start.3 = (bf16[96,2048]{1,0:T(8,128)(2,1)}, bf16[96,2048]{1,0:T(8,128)(2,1)}, u32[]{:S(2)}, u32[]{:S(2)}) collective-permute-start(bf16[96,2048]{1,0:T(8,128)(2,1)} %get-tuple-element.43), channel_id=1, source_target_pairs={{0,4},{2,6},{4,0},{6,2},{8,12},{10,14},{12,8},{14,10},{1,5},{3,7},... | collective-permute-start | bytes 1179656 | tf_op jit(solution)/shard_map/ppermute | solution.py:317
  13.6 1.9 %copy.20 = bf16[128,8,2,512]{3,1,2,0:T(8,128)(2,1)} copy(bf16[128,8,2,512]{3,2,1,0:T(2,128)(2,1)S(1)} %bitcast.53) | data formatting | bytes 4194304
  15.6 3.2 %project.5 = (bf16[96,1024]{1,0:T(8,128)(2,1)}, f32[96,1024]{1,0:T(8,128)}) custom-call(s32[1]{0:T(128)} %bitcast.3.side_ref, bf16[192,1024]{1,0:T(8,128)(2,1)} %states_hbm.3, bf16[1024,1024]{1,0:T(8,128)(2,1)} %bitcast.48), custom_call_target="tpu_custom_call" | custom-call | flops 402653184 | bytes 3080192 | tf_op jit(solution)/shard_map/project/pallas_call | solution.py:108
  21.2 2.0 %collective-permute-done.3 = bf16[96,2048]{1,0:T(8,128)(2,1)} collective-permute-done((bf16[96,2048]{1,0:T(8,128)(2,1)}, bf16[96,2048]{1,0:T(8,128)(2,1)}, u32[]{:S(2)}, u32[]{:S(2)}) %collective-permute-start.3) | collective-permute-done | bytes 393248 | tf_op jit(solution)/shard_map/ppermute | solution.py:317
  23.3 1.3 %convert_add_fusion = f32[96,2048]{1,0:T(8,128)S(1)} fusion(f32[96,2048]{1,0:T(8,128)} %get-tuple-element.45, bf16[96,2048]{1,0:T(8,128)(2,1)} %collective-permute-done.3), kind=kLoop, calls=%fused_computation.17 | loop fusion | flops 393216 | bytes 1966080 | tf_op jit(solution)/shard_map/add | solution.py:355
  24.6 2.5 %collective-permute-start.7 = (bf16[48,2048]{1,0:T(8,128)(2,1)S(1)}, bf16[48,2048]{1,0:T(8,128)(2,1)S(1)}, u32[]{:S(2)}, u32[]{:S(2)}) collective-permute-start(bf16[48,2048]{1,0:T(8,128)(2,1)S(1)} %fusion.28), channel_id=1, source_target_pairs={{0,8},{2,10},{4,12},{6,14},{8,0},{10,2},{12,4},{14,6},{1,9},{3,11}... | collective-permute-start | bytes 589832 | tf_op jit(solution)/shard_map/ppermute | solution.py:317
  27.2 2.5 %collective-permute-start.5 = (bf16[48,1024]{1,0:T(8,128)(2,1)S(1)}, bf16[48,1024]{1,0:T(8,128)(2,1)S(1)}, u32[]{:S(2)}, u32[]{:S(2)}) collective-permute-start(bf16[48,1024]{1,0:T(8,128)(2,1)S(1)} %bitcast.65), channel_id=1, source_target_pairs={{0,4},{2,6},{4,0},{6,2},{8,12},{10,14},{12,8},{14,10},{1,5},{3,7},... | collective-permute-start | bytes 294920 | tf_op jit(solution)/shard_map/ppermute | solution.py:317
  29.9 1.5 %collective-permute-start.4 = (bf16[24,2048]{1,0:T(8,128)(2,1)S(1)}, bf16[24,2048]{1,0:T(8,128)(2,1)S(1)}, u32[]{:S(2)}, u32[]{:S(2)}) collective-permute-start(bf16[24,2048]{1,0:T(8,128)(2,1)S(1)} %fusion.29), channel_id=1, source_target_pairs={{0,8},{2,10},{4,12},{6,14},{8,0},{10,2},{12,4},{14,6},{1,9},{3,11}... | collective-permute-start | bytes 294920 | tf_op jit(solution)/shard_map/ppermute | solution.py:317
  31.4 2.2 %collective-permute-done.5 = bf16[48,1024]{1,0:T(8,128)(2,1)S(1)} collective-permute-done((bf16[48,1024]{1,0:T(8,128)(2,1)S(1)}, bf16[48,1024]{1,0:T(8,128)(2,1)S(1)}, u32[]{:S(2)}, u32[]{:S(2)}) %collective-permute-start.5) | collective-permute-done | bytes 98336 | tf_op jit(solution)/shard_map/ppermute | solution.py:317
  33.6 3.8 %collective-permute-start.6 = (bf16[24,1024]{1,0:T(8,128)(2,1)S(1)}, bf16[24,1024]{1,0:T(8,128)(2,1)S(1)}, u32[]{:S(2)}, u32[]{:S(2)}) collective-permute-start(bf16[24,1024]{1,0:T(8,128)(2,1)S(1)} %fusion.31), channel_id=1, source_target_pairs={{0,8},{2,10},{4,12},{6,14},{8,0},{10,2},{12,4},{14,6},{1,9},{3,11}... | collective-permute-start | bytes 147464 | tf_op jit(solution)/shard_map/ppermute | solution.py:317
  37.5 1.7 %collective-permute-done.7 = bf16[48,2048]{1,0:T(8,128)(2,1)S(1)} collective-permute-done((bf16[48,2048]{1,0:T(8,128)(2,1)S(1)}, bf16[48,2048]{1,0:T(8,128)(2,1)S(1)}, u32[]{:S(2)}, u32[]{:S(2)}) %collective-permute-start.7) | collective-permute-done | bytes 196640 | tf_op jit(solution)/shard_map/ppermute | solution.py:317
  41.3 1.7 %attend.2 = bf16[24,2048]{1,0:T(8,128)(2,1)S(1)} custom-call(s32[24]{0:T(128)S(1)} %copy-done.1, f32[24,256]{1,0:T(8,128)S(1)} %pad_maximum_fusion.7.trig_ref, f32[24,2048]{1,0:T(8,128)S(1)} %dynamic-slice_bitcast_fusion.1.refs_0_, bf16[24,2048]{1,0:T(8,128)(2,1)S(1)} %collective-permute-done.4.refs_1_, f32[24,1024]{1,0:T(8,128)S(1)} %dynamic-slice_bitcast_fusion.2.refs_2_, ...), custom_call_target="tpu_custom_call" | custom-call | flops 50331648 | bytes 3145728 | tf_op jit(solution)/shard_map/attend/pallas_call | solution.py:211
  44.0 1.7 %attend.3 = bf16[24,2048]{1,0:T(8,128)(2,1)S(1)} custom-call(s32[24]{0:T(128)S(1)} %copy-done.1, f32[24,256]{1,0:T(8,128)S(1)} %pad_maximum_fusion.7.trig_ref, f32[24,2048]{1,0:T(8,128)S(1)} %dynamic-slice_bitcast_fusion.refs_0_, bf16[24,2048]{1,0:T(8,128)(2,1)S(1)} %collective-permute-done.8.refs_1_, f32[24,1024]{1,0:T(8,128)S(1)} %dynamic-slice_bitcast_fusion.2.refs_2_, ...), custom_call_target="tpu_custom_call" | custom-call | flops 50331648 | bytes 3145728 | tf_op jit(solution)/shard_map/attend/pallas_call | solution.py:211
  46.8 2.8 %collective-permute-start.9 = (bf16[24,4096]{1,0:T(8,128)(2,1)S(1)}, bf16[24,4096]{1,0:T(8,128)(2,1)S(1)}, u32[]{:S(2)}, u32[]{:S(2)}) collective-permute-start(bf16[24,4096]{1,0:T(8,128)(2,1)S(1)} %pad_maximum_fusion.4), channel_id=1, source_target_pairs={{0,8},{2,10},{4,12},{6,14},{8,0},{10,2},{12,4},{14,6},{1,9},{3,11}... | collective-permute-start | bytes 589832 | tf_op jit(solution)/shard_map/ppermute | solution.py:317
  49.6 1.8 %collective-permute-done.11 = bf16[24,4096]{1,0:T(8,128)(2,1)S(1)} collective-permute-done((bf16[24,4096]{1,0:T(8,128)(2,1)S(1)}, bf16[24,4096]{1,0:T(8,128)(2,1)S(1)}, u32[]{:S(2)}, u32[]{:S(2)}) %collective-permute-start.11) | collective-permute-done | bytes 196640 | tf_op jit(solution)/shard_map/ppermute | solution.py:317
  51.4 3.2 %collective-permute-done.10 = bf16[24,4096]{1,0:T(8,128)(2,1)S(1)} collective-permute-done((bf16[24,4096]{1,0:T(8,128)(2,1)S(1)}, bf16[24,4096]{1,0:T(8,128)(2,1)S(1)}, u32[]{:S(2)}, u32[]{:S(2)}) %collective-permute-start.10) | collective-permute-done | bytes 196640 | tf_op jit(solution)/shard_map/ppermute | solution.py:317
  57.6 1.9 %collective-permute-start.14 = (bf16[24,4096]{1,0:T(8,128)(2,1)S(1)}, bf16[24,4096]{1,0:T(8,128)(2,1)S(1)}, u32[]{:S(2)}, u32[]{:S(2)}) collective-permute-start(bf16[24,4096]{1,0:T(8,128)(2,1)S(1)} %collective-permute-done.9), channel_id=1, source_target_pairs={{0,2},{2,0},{4,6},{6,4},{8,10},{10,8},{12,14},{14,12},{1,3},{3,1},... | collective-permute-start | bytes 589832 | tf_op jit(solution)/shard_map/ppermute | solution.py:317
  59.7 3.5 %collective-permute-done.12 = bf16[24,4096]{1,0:T(8,128)(2,1)S(1)} collective-permute-done((bf16[24,4096]{1,0:T(8,128)(2,1)S(1)}, bf16[24,4096]{1,0:T(8,128)(2,1)S(1)}, u32[]{:S(2)}, u32[]{:S(2)}) %collective-permute-start.12) | collective-permute-done | bytes 196640 | tf_op jit(solution)/shard_map/ppermute | solution.py:317
  63.2 1.9 %collective-permute-start.15 = (bf16[24,4096]{1,0:T(8,128)(2,1)S(1)}, bf16[24,4096]{1,0:T(8,128)(2,1)S(1)}, u32[]{:S(2)}, u32[]{:S(2)}) collective-permute-start(bf16[24,4096]{1,0:T(8,128)(2,1)S(1)} %collective-permute-done.12), channel_id=1, source_target_pairs={{0,2},{2,0},{4,6},{6,4},{8,10},{10,8},{12,14},{14,12},{1,3},{3,1},... | collective-permute-start | bytes 589832 | tf_op jit(solution)/shard_map/ppermute | solution.py:317
  65.1 3.3 %collective-permute-done.13 = bf16[24,4096]{1,0:T(8,128)(2,1)S(1)} collective-permute-done((bf16[24,4096]{1,0:T(8,128)(2,1)S(1)}, bf16[24,4096]{1,0:T(8,128)(2,1)S(1)}, u32[]{:S(2)}, u32[]{:S(2)}) %collective-permute-start.13) | collective-permute-done | bytes 196640 | tf_op jit(solution)/shard_map/ppermute | solution.py:317
  68.4 2.1 %collective-permute-done.15 = bf16[24,4096]{1,0:T(8,128)(2,1)S(1)} collective-permute-done((bf16[24,4096]{1,0:T(8,128)(2,1)S(1)}, bf16[24,4096]{1,0:T(8,128)(2,1)S(1)}, u32[]{:S(2)}, u32[]{:S(2)}) %collective-permute-start.15) | collective-permute-done | bytes 196640 | tf_op jit(solution)/shard_map/ppermute | solution.py:317
  73.8 1.8 %collective-permute-start.17 = (bf16[96,64]{1,0:T(8,128)(2,1)S(1)}, bf16[96,64]{1,0:T(8,128)(2,1)S(1)}, u32[]{:S(2)}, u32[]{:S(2)}) collective-permute-start(bf16[96,64]{1,0:T(8,128)(2,1)S(1)} %add_convert_fusion), channel_id=1, source_target_pairs={{0,2},{2,0},{4,6},{6,4},{8,10},{10,8},{12,14},{14,12},{1,3},{3,1},... | collective-permute-start | bytes 36872 | tf_op jit(solution)/shard_map/ppermute | solution.py:317
  75.6 2.9 %fusion.4 = f32[120,1024]{1,0:T(8,128)S(1)} fusion(bf16[4096,1024]{1,0:T(8,128)(2,1)} %param.13, bf16[120,4096]{1,0:T(8,128)(2,1)S(1)} %constant_dynamic-update-slice_fusion), kind=kOutput, calls=%fused_computation.4 | convolution fusion | flops 503316480 | bytes 5177344 | tf_op jit(solution)/shard_map/dot_general | solution.py:391
  78.6 3.0 %fusion = f32[120,1024]{1,0:T(8,128)S(1)} fusion(bf16[4096,1024]{1,0:T(8,128)(2,1)} %param.13, bf16[120,4096]{1,0:T(8,128)(2,1)S(1)} %constant_dynamic-update-slice_fusion), kind=kOutput, calls=%fused_computation | convolution fusion | flops 503316480 | bytes 5177344 | tf_op jit(solution)/shard_map/dot_general | solution.py:391
  82.0 3.3 %collective-permute-start.20 = (bf16[96,64]{1,0:T(8,128)(2,1)S(1)}, bf16[96,64]{1,0:T(8,128)(2,1)S(1)}, u32[]{:S(2)}, u32[]{:S(2)}) collective-permute-start(bf16[96,64]{1,0:T(8,128)(2,1)S(1)} %add.157), channel_id=1, source_target_pairs={{0,12},{2,14},{4,8},{6,10},{8,4},{10,6},{12,0},{14,2},{1,13},{3,15... | collective-permute-start | bytes 36872 | tf_op jit(solution)/shard_map/ppermute | solution.py:317
  86.5 1.2 %collective-permute-done.20 = bf16[96,64]{1,0:T(8,128)(2,1)S(1)} collective-permute-done((bf16[96,64]{1,0:T(8,128)(2,1)S(1)}, bf16[96,64]{1,0:T(8,128)(2,1)S(1)}, u32[]{:S(2)}, u32[]{:S(2)}) %collective-permute-start.20) | collective-permute-done | bytes 12320 | tf_op jit(solution)/shard_map/ppermute | solution.py:317
  87.8 2.3 %collective-permute-done.19 = bf16[96,64]{1,0:T(8,128)(2,1)S(1)} collective-permute-done((bf16[96,64]{1,0:T(8,128)(2,1)S(1)}, bf16[96,64]{1,0:T(8,128)(2,1)S(1)}, u32[]{:S(2)}, u32[]{:S(2)}) %collective-permute-start.19) | collective-permute-done | bytes 12320 | tf_op jit(solution)/shard_map/ppermute | solution.py:317
  90.1 2.2 %copy-done = bf16[32,64,1024]{2,1,0:T(8,128)(2,1)S(1)} copy-done((bf16[32,64,1024]{2,1,0:T(8,128)(2,1)S(1)}, bf16[32,64,1024]{2,1,0:T(8,128)(2,1)}, u32[]{:S(2)}) %copy-start) | copy-done | bytes 4194328
  92.3 2.1 %finish.1 = bf16[96,1024]{1,0:T(8,128)(2,1)} custom-call(s32[2]{0:T(128)S(1)} %pad_add_fusion.place_ref, s32[96,1]{1,0:T(8,128)S(1)} %copy.19.slots_ref, bf16[96,64]{1,0:T(8,128)(2,1)S(1)} %add_add_fusion.low_ref, f32[96,1024]{1,0:T(8,128)S(1)} %pad_maximum_fusion.1.kept_ref, f32[96,1024]{1,0:T(8,128)S(1)} %collective-permute-done.21.sent_ref, ...), custom_call_target="tpu_custom_call" | custom-call | flops 402653184 | bytes 4194304 | tf_op jit(solution)/shard_map/finish/pallas_call | solution.py:269
  (118 shorter events, 14.5 us)
Async XLA Ops:
  4.4 15.6 %collective-permute-start = (bf16[96,2048]{1,0:T(8,128)(2,1)}, bf16[96,2048]{1,0:T(8,128)(2,1)}, u32[]{:S(2)}, u32[]{:S(2)}) collective-permute-start(bf16[96,2048]{1,0:T(8,128)(2,1)} %get-tuple-element.35), channel_id=1, source_target_pairs={{0,2},{2,0},{4,6},{6,4},{8,10},{10,8},{12,14},{14,12},{1,3},{3,1},... | collective-permute-start | bytes 1179656 | tf_op jit(solution)/shard_map/ppermute | solution.py:317
  11.9 7.5 %copy-start.7 = (s32[192]{0:T(256)S(1)}, s32[192]{0:T(256)}, u32[]{:S(2)}) copy-start(s32[192]{0:T(256)} %param.16) | copy-start | bytes 2308
  12.0 7.7 %copy-start.1 = (s32[24]{0:T(128)S(1)}, s32[24]{0:T(128)}, u32[]{:S(2)}) copy-start(s32[24]{0:T(128)} %lengths_ref.3) | copy-start | bytes 292
  12.0 8.0 %copy-start.3 = (f32[96,2048]{1,0:T(8,128)S(1)}, f32[96,2048]{1,0:T(8,128)}, u32[]{:S(2)}) copy-start(f32[96,2048]{1,0:T(8,128)} %get-tuple-element.34) | copy-start | bytes 2359300
  12.0 11.3 %collective-permute-start.3 = (bf16[96,2048]{1,0:T(8,128)(2,1)}, bf16[96,2048]{1,0:T(8,128)(2,1)}, u32[]{:S(2)}, u32[]{:S(2)}) collective-permute-start(bf16[96,2048]{1,0:T(8,128)(2,1)} %get-tuple-element.43), channel_id=1, source_target_pairs={{0,4},{2,6},{4,0},{6,2},{8,12},{10,14},{12,8},{14,10},{1,5},{3,7},... | collective-permute-start | bytes 1179656 | tf_op jit(solution)/shard_map/ppermute | solution.py:317
  15.6 25.7 %slice-start = ((s8[6291456]{0:T(1024)(128)(4,1)}), s8[2097152]{0:T(1024)(128)(4,1)S(1)}, s32[]{:S(2)}) async-start(s8[6291456]{0:T(1024)(128)(4,1)} %bitcast.45), calls=%async_computation | async-start | bytes 4194304
  18.8 8.3 %copy-start.4 = (f32[96,1024]{1,0:T(8,128)S(1)}, f32[96,1024]{1,0:T(8,128)}, u32[]{:S(2)}) copy-start(f32[96,1024]{1,0:T(8,128)} %get-tuple-element.47) | copy-start | bytes 1179652
  18.8 8.3 %collective-permute-start.2 = (bf16[96,1024]{1,0:T(8,128)(2,1)}, bf16[96,1024]{1,0:T(8,128)(2,1)S(1)}, u32[]{:S(2)}, u32[]{:S(2)}) collective-permute-start(bf16[96,1024]{1,0:T(8,128)(2,1)} %get-tuple-element.42), channel_id=1, source_target_pairs={{0,2},{2,0},{4,6},{6,4},{8,10},{10,8},{12,14},{14,12},{1,3},{3,1},... | collective-permute-start | bytes 589832 | tf_op jit(solution)/shard_map/ppermute | solution.py:317
  21.1 20.1 %slice-start.1 = ((s8[6291456]{0:T(1024)(128)(4,1)}), s8[4194304]{0:T(1024)(128)(4,1)S(1)}, s32[]{:S(2)}) async-start(s8[6291456]{0:T(1024)(128)(4,1)} %bitcast.45), calls=%async_computation.1 | async-start | bytes 8388608
  21.2 8.7 %collective-permute-start.1 = (bf16[48,2048]{1,0:T(8,128)(2,1)S(1)}, bf16[48,2048]{1,0:T(8,128)(2,1)S(1)}, u32[]{:S(2)}, u32[]{:S(2)}) collective-permute-start(bf16[48,2048]{1,0:T(8,128)(2,1)S(1)} %bitcast.64), channel_id=1, source_target_pairs={{0,4},{2,6},{4,0},{6,2},{8,12},{10,14},{12,8},{14,10},{1,5},{3,7},... | collective-permute-start | bytes 589832 | tf_op jit(solution)/shard_map/ppermute | solution.py:317
  24.6 14.6 %collective-permute-start.7 = (bf16[48,2048]{1,0:T(8,128)(2,1)S(1)}, bf16[48,2048]{1,0:T(8,128)(2,1)S(1)}, u32[]{:S(2)}, u32[]{:S(2)}) collective-permute-start(bf16[48,2048]{1,0:T(8,128)(2,1)S(1)} %fusion.28), channel_id=1, source_target_pairs={{0,8},{2,10},{4,12},{6,14},{8,0},{10,2},{12,4},{14,6},{1,9},{3,11}... | collective-permute-start | bytes 589832 | tf_op jit(solution)/shard_map/ppermute | solution.py:317
  27.2 6.3 %collective-permute-start.5 = (bf16[48,1024]{1,0:T(8,128)(2,1)S(1)}, bf16[48,1024]{1,0:T(8,128)(2,1)S(1)}, u32[]{:S(2)}, u32[]{:S(2)}) collective-permute-start(bf16[48,1024]{1,0:T(8,128)(2,1)S(1)} %bitcast.65), channel_id=1, source_target_pairs={{0,4},{2,6},{4,0},{6,2},{8,12},{10,14},{12,8},{14,10},{1,5},{3,7},... | collective-permute-start | bytes 294920 | tf_op jit(solution)/shard_map/ppermute | solution.py:317
  29.9 11.4 %collective-permute-start.4 = (bf16[24,2048]{1,0:T(8,128)(2,1)S(1)}, bf16[24,2048]{1,0:T(8,128)(2,1)S(1)}, u32[]{:S(2)}, u32[]{:S(2)}) collective-permute-start(bf16[24,2048]{1,0:T(8,128)(2,1)S(1)} %fusion.29), channel_id=1, source_target_pairs={{0,8},{2,10},{4,12},{6,14},{8,0},{10,2},{12,4},{14,6},{1,9},{3,11}... | collective-permute-start | bytes 294920 | tf_op jit(solution)/shard_map/ppermute | solution.py:317
  33.6 7.7 %collective-permute-start.6 = (bf16[24,1024]{1,0:T(8,128)(2,1)S(1)}, bf16[24,1024]{1,0:T(8,128)(2,1)S(1)}, u32[]{:S(2)}, u32[]{:S(2)}) collective-permute-start(bf16[24,1024]{1,0:T(8,128)(2,1)S(1)} %fusion.31), channel_id=1, source_target_pairs={{0,8},{2,10},{4,12},{6,14},{8,0},{10,2},{12,4},{14,6},{1,9},{3,11}... | collective-permute-start | bytes 147464 | tf_op jit(solution)/shard_map/ppermute | solution.py:317
  39.3 4.7 %collective-permute-start.8 = (bf16[24,2048]{1,0:T(8,128)(2,1)S(1)}, bf16[24,2048]{1,0:T(8,128)(2,1)S(1)}, u32[]{:S(2)}, u32[]{:S(2)}) collective-permute-start(bf16[24,2048]{1,0:T(8,128)(2,1)S(1)} %fusion.30), channel_id=1, source_target_pairs={{0,2},{2,0},{4,6},{6,4},{8,10},{10,8},{12,14},{14,12},{1,3},{3,1},... | collective-permute-start | bytes 294920 | tf_op jit(solution)/shard_map/ppermute | solution.py:317
  41.3 13.9 %slice-start.3 = ((s8[8388608]{0:T(1024)(128)(4,1)}), s8[4194304]{0:T(1024)(128)(4,1)S(1)}, s32[]{:S(2)}) async-start(s8[8388608]{0:T(1024)(128)(4,1)} %bitcast.66), calls=%async_computation.3 | async-start | bytes 8388608
  43.0 11.7 %copy-start.9 = (bf16[4,64,4096]{2,1,0:T(8,128)(2,1)S(1)}, bf16[4,64,4096]{2,1,0:T(8,128)(2,1)}, u32[]{:S(2)}) copy-start(bf16[4,64,4096]{2,1,0:T(8,128)(2,1)} %param.18) | copy-start | bytes 6291460
  43.0 12.1 %slice-start.4 = ((s8[8388608]{0:T(1024)(128)(4,1)}), s8[4194304]{0:T(1024)(128)(4,1)S(1)}, s32[]{:S(2)}) async-start(s8[8388608]{0:T(1024)(128)(4,1)} %bitcast.66), calls=%async_computation.4 | async-start | bytes 8388608
  45.7 5.7 %collective-permute-start.11 = (bf16[24,4096]{1,0:T(8,128)(2,1)S(1)}, bf16[24,4096]{1,0:T(8,128)(2,1)S(1)}, u32[]{:S(2)}, u32[]{:S(2)}) collective-permute-start(bf16[24,4096]{1,0:T(8,128)(2,1)S(1)} %pad_maximum_fusion.4), channel_id=1, source_target_pairs={{0,2},{2,0},{4,6},{6,4},{8,10},{10,8},{12,14},{14,12},{1,3},{3,1},... | collective-permute-start | bytes 589832 | tf_op jit(solution)/shard_map/ppermute | solution.py:317
  46.7 7.9 %collective-permute-start.10 = (bf16[24,4096]{1,0:T(8,128)(2,1)S(1)}, bf16[24,4096]{1,0:T(8,128)(2,1)S(1)}, u32[]{:S(2)}, u32[]{:S(2)}) collective-permute-start(bf16[24,4096]{1,0:T(8,128)(2,1)S(1)} %pad_maximum_fusion.4), channel_id=1, source_target_pairs={{0,4},{2,6},{4,0},{6,2},{8,12},{10,14},{12,8},{14,10},{1,5},{3,7},... | collective-permute-start | bytes 589832 | tf_op jit(solution)/shard_map/ppermute | solution.py:317
  46.8 10.7 %collective-permute-start.9 = (bf16[24,4096]{1,0:T(8,128)(2,1)S(1)}, bf16[24,4096]{1,0:T(8,128)(2,1)S(1)}, u32[]{:S(2)}, u32[]{:S(2)}) collective-permute-start(bf16[24,4096]{1,0:T(8,128)(2,1)S(1)} %pad_maximum_fusion.4), channel_id=1, source_target_pairs={{0,8},{2,10},{4,12},{6,14},{8,0},{10,2},{12,4},{14,6},{1,9},{3,11}... | collective-permute-start | bytes 589832 | tf_op jit(solution)/shard_map/ppermute | solution.py:317
  57.0 15.7 %copy-start.5 = (f32[72,1024]{1,0:T(8,128)}, f32[72,1024]{1,0:T(8,128)S(1)}, u32[]{:S(2)}) copy-start(f32[72,1024]{1,0:T(8,128)S(1)} %fusion.8) | copy-start | bytes 884740
  57.5 5.7 %collective-permute-start.12 = (bf16[24,4096]{1,0:T(8,128)(2,1)S(1)}, bf16[24,4096]{1,0:T(8,128)(2,1)S(1)}, u32[]{:S(2)}, u32[]{:S(2)}) collective-permute-start(bf16[24,4096]{1,0:T(8,128)(2,1)S(1)} %collective-permute-done.9), channel_id=1, source_target_pairs={{0,4},{2,6},{4,0},{6,2},{8,12},{10,14},{12,8},{14,10},{1,5},{3,7},... | collective-permute-start | bytes 589832 | tf_op jit(solution)/shard_map/ppermute | solution.py:317
  57.6 10.8 %collective-permute-start.14 = (bf16[24,4096]{1,0:T(8,128)(2,1)S(1)}, bf16[24,4096]{1,0:T(8,128)(2,1)S(1)}, u32[]{:S(2)}, u32[]{:S(2)}) collective-permute-start(bf16[24,4096]{1,0:T(8,128)(2,1)S(1)} %collective-permute-done.9), channel_id=1, source_target_pairs={{0,2},{2,0},{4,6},{6,4},{8,10},{10,8},{12,14},{14,12},{1,3},{3,1},... | collective-permute-start | bytes 589832 | tf_op jit(solution)/shard_map/ppermute | solution.py:317
  59.5 8.9 %collective-permute-start.13 = (bf16[24,4096]{1,0:T(8,128)(2,1)S(1)}, bf16[24,4096]{1,0:T(8,128)(2,1)S(1)}, u32[]{:S(2)}, u32[]{:S(2)}) collective-permute-start(bf16[24,4096]{1,0:T(8,128)(2,1)S(1)} %collective-permute-done.10), channel_id=1, source_target_pairs={{0,2},{2,0},{4,6},{6,4},{8,10},{10,8},{12,14},{14,12},{1,3},{3,1},... | collective-permute-start | bytes 589832 | tf_op jit(solution)/shard_map/ppermute | solution.py:317
  63.2 7.3 %collective-permute-start.15 = (bf16[24,4096]{1,0:T(8,128)(2,1)S(1)}, bf16[24,4096]{1,0:T(8,128)(2,1)S(1)}, u32[]{:S(2)}, u32[]{:S(2)}) collective-permute-start(bf16[24,4096]{1,0:T(8,128)(2,1)S(1)} %collective-permute-done.12), channel_id=1, source_target_pairs={{0,2},{2,0},{4,6},{6,4},{8,10},{10,8},{12,14},{14,12},{1,3},{3,1},... | collective-permute-start | bytes 589832 | tf_op jit(solution)/shard_map/ppermute | solution.py:317
  72.5 1.3 %collective-permute-start.16 = (f32[96,64]{1,0:T(8,128)S(1)}, f32[96,64]{1,0:T(8,128)S(1)}, u32[]{:S(2)}, u32[]{:S(2)}) collective-permute-start(f32[96,64]{1,0:T(8,128)S(1)} %constant_dynamic-slice_fusion), channel_id=1, source_target_pairs={{0,1},{1,0},{2,3},{3,2},{4,5},{5,4},{6,7},{7,6},{8,9},{9,8},{10,11... | collective-permute-start | bytes 73736 | tf_op jit(solution)/shard_map/ppermute | solution.py:320
  73.8 4.7 %collective-permute-start.17 = (bf16[96,64]{1,0:T(8,128)(2,1)S(1)}, bf16[96,64]{1,0:T(8,128)(2,1)S(1)}, u32[]{:S(2)}, u32[]{:S(2)}) collective-permute-start(bf16[96,64]{1,0:T(8,128)(2,1)S(1)} %add_convert_fusion), channel_id=1, source_target_pairs={{0,2},{2,0},{4,6},{6,4},{8,10},{10,8},{12,14},{14,12},{1,3},{3,1},... | collective-permute-start | bytes 36872 | tf_op jit(solution)/shard_map/ppermute | solution.py:317
  81.8 8.3 %collective-permute-start.21 = (f32[96,1024]{1,0:T(8,128)S(1)}, f32[96,1024]{1,0:T(8,128)S(1)}, u32[]{:S(2)}, u32[]{:S(2)}) collective-permute-start(f32[96,1024]{1,0:T(8,128)S(1)} %pad_maximum_fusion.2), channel_id=1, source_target_pairs={{0,1},{1,0},{2,3},{3,2},{4,5},{5,4},{6,7},{7,6},{8,9},{9,8},{10,11... | collective-permute-start | bytes 1179656 | tf_op jit(solution)/shard_map/ppermute | solution.py:320
  82.0 5.7 %collective-permute-start.20 = (bf16[96,64]{1,0:T(8,128)(2,1)S(1)}, bf16[96,64]{1,0:T(8,128)(2,1)S(1)}, u32[]{:S(2)}, u32[]{:S(2)}) collective-permute-start(bf16[96,64]{1,0:T(8,128)(2,1)S(1)} %add.157), channel_id=1, source_target_pairs={{0,12},{2,14},{4,8},{6,10},{8,4},{10,6},{12,0},{14,2},{1,13},{3,15... | collective-permute-start | bytes 36872 | tf_op jit(solution)/shard_map/ppermute | solution.py:317
  85.4 4.7 %collective-permute-start.19 = (bf16[96,64]{1,0:T(8,128)(2,1)S(1)}, bf16[96,64]{1,0:T(8,128)(2,1)S(1)}, u32[]{:S(2)}, u32[]{:S(2)}) collective-permute-start(bf16[96,64]{1,0:T(8,128)(2,1)S(1)} %add.157), channel_id=1, source_target_pairs={{0,8},{2,10},{4,12},{6,14},{8,0},{10,2},{12,4},{14,6},{1,9},{3,11}... | collective-permute-start | bytes 36872 | tf_op jit(solution)/shard_map/ppermute | solution.py:317
  85.7 4.4 %collective-permute-start.18 = (bf16[96,64]{1,0:T(8,128)(2,1)S(1)}, bf16[96,64]{1,0:T(8,128)(2,1)S(1)}, u32[]{:S(2)}, u32[]{:S(2)}) collective-permute-start(bf16[96,64]{1,0:T(8,128)(2,1)S(1)} %add.157), channel_id=1, source_target_pairs={{0,4},{2,6},{4,0},{6,2},{8,12},{10,14},{12,8},{14,10},{1,5},{3,7},... | collective-permute-start | bytes 36872 | tf_op jit(solution)/shard_map/ppermute | solution.py:317
  (5 other events, 22.1 us)
